TPU v7x, 512 devices: a whole 4x8x8 slice. The times are simulated.
512 devices in a mesh: col: 8 (over y_lo, core), dev: 64 (over y_hi, z, x).
Axes of the slice: x: 4, y: 8 (y_hi: 2, y_lo: 4; y = y_hi * 4 + y_lo), z: 8, core: 2. Of those that a mesh axis runs over, the one named last changes fastest.
Arguments:
- factor_a: float32 [1536, 16, 512], P('dev'), may hold values from -1 to 1
- factor_b: float32 [1536, 64, 512], P('dev', 'col'), may hold values from -1 to 1
- factor_occ: float32 [1536, 16, 512], P('dev'), may hold values from -1 to 1
- singles_a: float32 [16, 16], replicated, may hold values from -1.5 to 1.5
- singles_b: float32 [16, 64], P(None, 'col'), may hold values from -1.5 to 1.5
- doubles: bfloat16 [512, 512, 256], P('col', 'dev'), may hold values from -0.023925781 to 0.023925781
- orbital_a: float32 [16], P('col'), may hold values from 0.2 to 3
- orbital_b: float32 [64], P('dev'), may hold values from 0.2 to 3
- orbital_occ: float32 [16], replicated, may hold values from -2 to -0.3
Outputs:
- update: float32 [16, 64, 256], P('col', 'dev')
All inputs are finite; a program needn't handle non-finite values.
Results may differ from a plain program's by a relative error of at most 0.0049.
Values may be sent and summed in bfloat16 or wider, within the bound.
A program may use at most 64 MiB of HBM per device.

v0:
```python
import jax
import jax.numpy as jnp
from jax import lax
from jax.sharding import PartitionSpec as P


def body(
    factor_a, factor_b, factor_occ, singles_a, singles_b, doubles, orbital_a, orbital_b, orbital_occ
):
    highest = lax.Precision.HIGHEST
    c_tile = doubles.shape[0]
    d_tile = doubles.shape[1]
    pair_count = doubles.shape[2]
    shard_rows = factor_a.shape[0]
    a_rows = factor_a.shape[1]
    d_groups = factor_b.shape[2] // d_tile
    col_index = lax.axis_index("col")
    occ_tile = lax.dynamic_slice_in_dim(factor_occ, col_index * c_tile, c_tile, 2)
    a_tile = lax.dynamic_slice_in_dim(factor_a, col_index * c_tile, c_tile, 2)
    dressed_a = (a_tile - jnp.einsum("ka,qkc->qac", singles_a, occ_tile, precision=highest)).astype(
        jnp.bfloat16
    )
    dressed_a = dressed_a.reshape(shard_rows, a_rows * c_tile)
    dressed_b = (
        factor_b - jnp.einsum("kb,qkd->qbd", singles_b, factor_occ, precision=highest)
    ).astype(jnp.bfloat16)
    rows_all = lax.all_gather(dressed_b, "col", axis=1, tiled=True)
    b_rows_all = rows_all.shape[1]
    grouped = rows_all.reshape(shard_rows, b_rows_all, d_groups, d_tile)
    grouped = jnp.transpose(grouped, (0, 2, 1, 3)).reshape(
        shard_rows, d_groups, b_rows_all * d_tile
    )
    moved = lax.all_to_all(grouped, "dev", split_axis=1, concat_axis=0, tiled=True)
    whole_b = moved.reshape(moved.shape[0], -1)
    b_rows_all = whole_b.shape[1] // d_tile
    contract_first = (((0,), (0,)), ((), ()))
    whole_a = lax.all_gather(dressed_a, "dev", axis=0, tiled=True)
    integral = lax.dot_general(whole_a, whole_b, contract_first, preferred_element_type=jnp.float32)
    integral = integral.astype(jnp.bfloat16).reshape(a_rows, c_tile, b_rows_all, d_tile)
    integral = jnp.transpose(integral, (0, 2, 1, 3)).reshape(a_rows * b_rows_all, c_tile * d_tile)
    partial_value = jnp.dot(
        integral, doubles.reshape(c_tile * d_tile, pair_count), preferred_element_type=jnp.float32
    )
    partial_value = partial_value.reshape(a_rows, b_rows_all, pair_count)
    reduced = lax.psum_scatter(partial_value, "dev", scatter_dimension=1, tiled=True)
    total = lax.psum_scatter(reduced, "col", scatter_dimension=0, tiled=True)
    pair_energy = (orbital_occ[:, None] + orbital_occ[None, :]).reshape(-1)
    denominator = orbital_a[:, None, None] + orbital_b[None, :, None] - pair_energy[None, None, :]
    return total / denominator


def solution(mesh):
    return jax.shard_map(
        body,
        mesh=mesh,
        in_specs=(
            P("dev", None, None),
            P("dev", "col", None),
            P("dev", None, None),
            P(),
            P(None, "col"),
            P("col", "dev", None),
            P("col"),
            P("dev"),
            P(),
        ),
        out_specs=P("col", "dev", None),
        check_vma=False,
    )
```

profile of v0, /device:TPU:1, one launch (start us, length us, event | category | flops | bytes accessed | tf_op | source)
XLA Modules:
  0.0 714.7 jit_solution(8249692002151963328)
XLA Ops:
  6.5 1.1 copy-done
  7.7 2.2 fusion.1
  9.9 0.0 all-gather.3.cloned.1.call-start
  10.0 1.4 fusion.3
  11.3 0.7 reshape.86
  12.1 0.0 reduce-scatter.2.cloned.1.call-start
  12.1 42.0 %all-gather.5.cloned.1.call-done = bf16[24,64,512]{2,1,0:T(8,128)(2,1)} async-done(((bf16[24,8,512]{2,1,0:T(8,128)(2,1)}), bf16[24,64,512]{2,1,0:T(8,128)(2,1)}) %all-gather.5.cloned.1.call-update) | async-done | bytes 1572880 | tf_op jit(solution)/shard_map/all_gather | solution.py:27
  54.2 4.1 copy.21
  58.3 5.4 copy.22
  63.7 3.9 copy.23
  67.6 53.7 %all_to_all.15 = bf16[24,64,512]{2,0,1:T(8,128)(2,1)} all-to-all(bf16[24,64,512]{2,0,1:T(8,128)(2,1)S(1)} %copy.23), channel_id=1, replica_groups=mesh['col'=8,'dev'=64] {'dev'}, dimensions={1} | all-to-all | bytes 3145728 | tf_op jit(solution)/shard_map/all_to_all | solution.py:33
  121.3 96.4 %all-gather.3.cloned.1.call-done = bf16[1536,1024]{1,0:T(8,128)(2,1)} async-done(((bf16[24,1024]{1,0:T(8,128)(2,1)}), bf16[1536,1024]{1,0:T(8,128)(2,1)}) %all-gather.3.cloned.1.call-update) | async-done | bytes 3145744 | tf_op jit(solution)/shard_map/all_gather | solution.py:37
  217.7 4.2 convolution_convert_fusion
  221.9 1.3 copy.24
  223.2 2.9 reshape.90
  226.2 6.6 copy.29
  232.7 6.8 convolution_bitcast_fusion
  239.6 0.1 broadcast_add_fusion
  239.7 0.1 add.46
  240.4 1.3 dynamic-slice
  242.4 389.7 %reduce-scatter.2.cloned.1.call-done = f32[16,1,256]{2,0,1:T(8,128)} async-done(((f32[16,64,256]{2,0,1:T(8,128)}), f32[16,1,256]{2,0,1:T(8,128)}) %reduce-scatter.2.cloned.1.call-update) | async-done | bytes 16400 | tf_op jit(solution)/shard_map/reduce_scatter | solution.py:45
  632.1 0.7 copy.27
  632.8 74.7 %all-reduce = f32[16,1,256]{2,1,0:T(1,128)S(1)} all-reduce(f32[16,1,256]{2,1,0:T(1,128)S(1)} %copy.27), channel_id=3, replica_groups=mesh['col'=8,'dev'=64] {'col'}, use_global_device_ids=true, to_apply=%region_1.0.clone | all-reduce | flops 4096 | bytes 32768
  707.5 0.7 dynamic-slice_divide_fusion
  (12 shorter events, 0.1 us)
Async XLA Ops:
  6.5 1.1 copy-start
  6.5 47.6 %all-gather.5.cloned.1.call-start = ((), (), s32[]{:S(2)}) async-start(), calls=%async_computation.3 | async-start | bytes 1769472 | tf_op jit(solution)/shard_map/all_gather | solution.py:27
  9.9 207.8 %all-gather.3.cloned.1.call-start = ((), (), s32[]{:S(2)}) async-start(), calls=%async_computation.2 | async-start | bytes 3194880 | tf_op jit(solution)/shard_map/all_gather | solution.py:37
  12.1 620.0 %reduce-scatter.2.cloned.1.call-start = ((), (), s32[]{:S(2)}) async-start(), calls=%async_computation.4 | async-start | bytes 1064960 | tf_op jit(solution)/shard_map/reduce_scatter | solution.py:45
  226.2 6.6 copy-start.1
  232.7 6.8 copy-start.2
  232.7 9.6 %copy-start.3 = (f32[2]{0:T(128)S(1)}, f32[2]{0:T(128)}, u32[]{:S(2)}) copy-start(f32[2]{0:T(128)} %param.15) | copy-start | bytes 28
Sparse Core Ops, SparseCore 0:
  10.0 44.0 all-gather.4
  58.7 158.9 all-gather.2
  239.7 392.3 reduce-scatter.1
where the time goes:
time: 715 us
  waiting for transfers between devices  528 us (74%)
  blocking collectives  128 us (18%)
  local copies, waits for them, and re-layouts  28.2 us (4%)
  matrix products  14.5 us (2%)
  between operations  14.5 us (2%)
    reduce_scatter x1, waiting for transfers between devices, body(): lax.psum_scatter(partial_value, 'dev', scatter_dimension=1, tiled=True)  390 us
    all_gather x1, waiting for transfers between devices, body(): whole_a = lax.all_gather(dressed_a, 'dev', axis=0, tiled=True)  96.4 us
    unnamed x1, blocking collectives  74.7 us
    all_to_all x1, blocking collectives, body(): lax.all_to_all(grouped, 'dev', split_axis=1, concat_axis=0, tiled=True)  53.7 us
    all_gather x1, waiting for transfers between devices, body(): rows_all = lax.all_gather(dressed_b, 'col', axis=1, tiled=True)  42 us
  transfers between devices with their start and end apart: 3, of which 3 were waited for; matrix products, arithmetic and copies ran while one was open for 2% of the time, Pallas kernels for 0%

commit v1 on v0

v1 whole, which is shorter than its diff:
```python
import jax
import jax.numpy as jnp
from jax import lax
from jax.experimental import pallas as pl
from jax.experimental.pallas import tpu as pltpu
from jax.sharding import PartitionSpec as P

MESH = pl.DeviceIdType.MESH
F32 = jnp.float32
BF16 = jnp.bfloat16
HIGHEST = lax.Precision.HIGHEST
NH, NZ, NX, NL, NK = 2, 8, 4, 4, 2


def lanes_of(shape):
    return lax.broadcasted_iota(jnp.int32, shape, len(shape) - 1)


def rows_of(shape):
    return lax.broadcasted_iota(jnp.int32, shape, 0)


def spread(singles, rows):
    pick = (rows_of((rows * 8, rows)) // 8 == lanes_of((rows * 8, rows))).astype(F32)
    across = (rows_of((16, 128)) == lanes_of((16, 128)) % 16).astype(F32)
    first = lax.dot_general(pick, singles, (((1,), (1,)), ((), ())), precision=HIGHEST)
    full = jnp.dot(first, across, precision=HIGHEST)
    same = rows_of((rows * 8, 128)) % 8 == lanes_of((rows * 8, 128)) // 16
    return jnp.where(same, full, 0.0)


def strided(ref, start, size, stride):
    tiles = [ref[t, pl.ds(start, size, stride=stride), :] for t in range(ref.shape[0])]
    return jnp.concatenate(tiles, axis=1)


def put(ref, value):
    for t in range(ref.shape[0]):
        ref[t] = value[:, t * 128 : (t + 1) * 128]


def kernel(
    fa, fb, fo, sa, sb, tau, oa, ob, oo, out,
    fo_v, fb_v, fa_v, tau_v, tf_v,
    b1_send, b1_recv, b2_send, b_all, bt_all,
    a_blk, a_mir, a_all, t_all, integral, acc_p, acc_o,
    c_send, c_recv, x_send, x_recv, s_v, z_send, z_recv, s2_v, y_send, y_recv,
    load_sem, b1_ss, b1_rs, b2_ss, b2_rs, fw_ss, fw_rs, am_ss, am_rs, a_ss, a_rs,
    t_ss, t_rs, c_ss, c_rs, x_ss, x_rs, z_ss, z_rs, y_ss, y_rs,
):
    col = lax.axis_index("col")
    dev = lax.axis_index("dev")
    l, k = col // NK, col % NK
    h, z, x = dev // (NZ * NX), (dev // NX) % NZ, dev % NX

    def col_id(l_, k_):
        return l_ * NK + k_

    def dev_id(h_, z_, x_):
        return (h_ * NZ + z_) * NX + x_

    def at(h_=h, z_=z, x_=x, l_=l, k_=k):
        return (col_id(l_, k_), dev_id(h_, z_, x_))

    def remote(src, dst, ss, rs, target):
        return pltpu.make_async_remote_copy(
            src_ref=src, dst_ref=dst, send_sem=ss, recv_sem=rs, device_id=target, device_id_type=MESH
        )

    def wait_recv(dst, ss, rs):
        remote(dst, dst, ss, rs, at(k_=1 - k)).wait_recv()

    hl, ml = h, NL - 1 - l
    own_lanes = pl.ds(pl.multiple_of(l * 128, 128), 128)
    mir_lanes = pl.ds(pl.multiple_of(ml * 128, 128), 128)
    loads = [
        pltpu.make_async_copy(fo, fo_v, load_sem.at[0]),
        pltpu.make_async_copy(fb.at[:, 0:128], fb_v.at[0], load_sem.at[1]),
        pltpu.make_async_copy(fa.at[:, mir_lanes], fa_v.at[0], load_sem.at[2]),
        pltpu.make_async_copy(fa.at[:, own_lanes], fa_v.at[1], load_sem.at[3]),
        pltpu.make_async_copy(tau, tau_v, load_sem.at[4]),
    ] + [
        pltpu.make_async_copy(fb.at[:, t * 128 : (t + 1) * 128], fb_v.at[t], load_sem.at[4 + t])
        for t in range(1, 4)
    ]
    for load in loads:
        load.start()

    z_peers = [at(z_=(z + s) % NZ) for s in range(1, NZ)]
    x_peers = [at(x_=(x + s) % NX) for s in range(1, NX)]
    y_offsets = [(dh, dl) for dh in range(NH) for dl in range(NL) if (dh, dl) != (0, 0)]
    y_peers = [at(h_=(h + dh) % NH, l_=(l + dl) % NL) for dh, dl in y_offsets]
    sibling = at(k_=1 - k)
    barrier = pltpu.get_barrier_semaphore()
    everyone = z_peers + x_peers + y_peers + [sibling]
    for peer in everyone:
        pl.semaphore_signal(barrier, inc=1, device_id=peer, device_id_type=MESH)

    lane128 = lanes_of((1, 128))
    low = lane128 < 64

    pb = spread(sb[...], 8)
    pa = spread(sa[...], 16)
    loads[0].wait()
    for n in (1, 5, 6, 7):
        loads[n].wait()
    parts = [[] for _ in range(8)]
    for g in range(3):
        prod = jnp.dot(pb, fo_v[g * 128 : (g + 1) * 128, :], precision=HIGHEST)
        for b in range(8):
            parts[b].append(strided(fb_v, g * 64 + b, 8, 8) - prod[b * 8 : (b + 1) * 8])
    stacked = []
    for b in range(8):
        whole = jnp.concatenate(parts[b], axis=0)
        stacked.append(jnp.concatenate([whole[:, t * 128 : (t + 1) * 128] for t in range(4)], axis=0))
    quarter = lane128 % 64 < 32
    for bq in range(2):
        x0, x1, x2, x3 = stacked[bq * 4 : bq * 4 + 4]
        u0 = jnp.where(low, x0, pltpu.roll(x2, 64, 1))
        u2 = jnp.where(low, pltpu.roll(x0, 64, 1), x2)
        u1 = jnp.where(low, x1, pltpu.roll(x3, 64, 1))
        u3 = jnp.where(low, pltpu.roll(x1, 64, 1), x3)
        ys = [
            jnp.where(quarter, u0, pltpu.roll(u1, 32, 1)),
            jnp.where(quarter, pltpu.roll(u0, 96, 1), u1),
            jnp.where(quarter, u2, pltpu.roll(u3, 32, 1)),
            jnp.where(quarter, pltpu.roll(u2, 96, 1), u3),
        ]
        for tt in range(2):
            for j in range(4):
                y = ys[j]
                piece = jnp.concatenate(
                    [y[tt * 24 : tt * 24 + 24], y[(2 + tt) * 24 : (2 + tt) * 24 + 24]], axis=0
                )
                b1_send[tt * 4 + j, :, bq * 128 : (bq + 1) * 128] = piece.astype(BF16)

    pl.semaphore_wait(barrier, len(everyone))

    b1 = []
    for s in range(1, NZ):
        zt = (z + s) % NZ
        b1.append(remote(b1_send.at[zt], b1_recv.at[z], b1_ss.at[s], b1_rs.at[s], at(z_=zt)))
        b1[-1].start()
    b1_recv[z] = b1_send[z]

    def dress_a(which):
        half = [[], []]
        for g in range(3):
            lanes = pl.ds(pl.multiple_of((ml if which == 0 else l) * 128, 128), 128)
            prod = jnp.dot(pa, fo_v[g * 128 : (g + 1) * 128, lanes], precision=HIGHEST)
            rows = []
            for a in range(16):
                d = fa_v[which, pl.ds(g * 128 + a, 8, stride=16), :] - prod[a * 8 : (a + 1) * 8]
                rows.append(d)
            for ah in range(2):
                lane_tiles = []
                for pair in range(4):
                    d0, d1 = rows[ah * 8 + pair * 2], rows[ah * 8 + pair * 2 + 1]
                    r0, r1 = pltpu.roll(d0, 64, 1), pltpu.roll(d1, 64, 1)
                    e0 = jnp.where(k == 0, d0, r0)
                    e1 = jnp.where(k == 0, r1, d1)
                    lane_tiles.append(jnp.where(low, e0, e1))
                half[ah].append(jnp.concatenate(lane_tiles, axis=1))
        return jnp.concatenate(half[0] + half[1], axis=0).astype(BF16)

    loads[2].wait()
    a_mir[...] = dress_a(0)
    mirror = at(h_=1 - h, l_=ml)
    am = remote(a_mir, a_blk.at[z, h], am_ss.at[0], am_rs.at[0], mirror)
    am.start()
    loads[3].wait()
    a_blk[z, h] = dress_a(1)

    right, left = at(z_=(z + 1) % NZ), at(z_=(z + NZ - 1) % NZ)
    a_sent = []

    def a_send(way, step, part):
        zs = (z - step + NZ) % NZ if way == 0 else (z + step) % NZ
        hs = h if part == 0 else 1 - h
        ref = a_blk.at[zs, hs]
        n = step * 2 + part
        copy = remote(ref, ref, a_ss.at[way, n], a_rs.at[way, n], right if way == 0 else left)
        copy.start()
        a_sent.append(copy)

    def a_wait(way, step, part):
        zs = (z - step - 1 + NZ) % NZ if way == 0 else (z + step + 1) % NZ
        hs = h if part == 0 else 1 - h
        n = step * 2 + part
        wait_recv(a_blk.at[zs, hs], a_ss.at[way, n], a_rs.at[way, n])

    a_send(0, 0, 0)
    a_send(1, 0, 0)

    loads[4].wait()
    put(tf_v, tau_v[...].astype(F32))
    for d in range(8):
        for e in range(2):
            t_all[x, d * 64 + e * 32 : d * 64 + e * 32 + 32, :] = strided(
                tf_v, e * 256 + d, 32, 8
            ).astype(BF16)
    ts = []
    for s in range(1, NX):
        ref = t_all.at[x]
        ts.append(remote(ref, ref, t_ss.at[s], t_rs.at[s], at(x_=(x + s) % NX)))
        ts[-1].start()

    for s in range(1, NZ):
        wait_recv(b1_recv.at[(z - s + NZ) % NZ], b1_ss.at[s], b1_rs.at[s])
    ri, ci = rows_of((256, 256)), lanes_of((256, 256))
    perm = ((ri // 8 == ci % 32) & (ri % 8 == ci // 32)).astype(BF16)
    blocks = [b1_recv[zz].astype(F32) for zz in range(NZ)]
    for hd in range(NH):
        rows = [blk[hd * 24 : hd * 24 + 24] for blk in blocks] + [jnp.zeros((64, 256), F32)]
        stack = jnp.concatenate(rows, axis=0).astype(BF16)
        bt = lax.dot_general(perm, stack, (((1,), (1,)), ((), ())), preferred_element_type=F32)
        rest = bt[:, 128:]
        fold = jnp.where(low, rest[:128], pltpu.roll(rest[128:], 64, 1))
        b2_send[hd, 0:256] = bt[:, :128].astype(BF16)
        b2_send[hd, 256:384] = fold.astype(BF16)
    b2 = []
    for n, (dh, dl) in enumerate(y_offsets):
        hd, ld = (h + dh) % NH, (l + dl) % NL
        b2.append(
            remote(b2_send.at[hd], b_all.at[h, col], b2_ss.at[n], b2_rs.at[n], at(h_=hd, l_=ld))
        )
        b2[-1].start()
    fw = [remote(b2_send.at[h], b_all.at[h, col], fw_ss.at[7], fw_rs.at[7], sibling)]
    fw[0].start()
    b_all[h, col] = b2_send[h]

    wait_recv(a_blk.at[z, 1 - h], am_ss.at[0], am_rs.at[0])
    a_send(0, 0, 1)
    a_send(1, 0, 1)
    for step in range(3):
        for part in range(2):
            for way in range(2):
                a_wait(way, step, part)
                if step < 2 or way == part:
                    a_send(way, step + 1, part)

    for n, (dh, dl) in enumerate(y_offsets):
        hs, ls = (h + dh) % NH, (l - dl + NL) % NL
        ref = b_all.at[hs, col_id(ls, k)]
        wait_recv(ref, b2_ss.at[n], b2_rs.at[n])
        fw.append(remote(ref, ref, fw_ss.at[n], fw_rs.at[n], sibling))
        fw[-1].start()

    a_wait(0, 3, 0)
    a_wait(1, 3, 1)
    for zp in range(4):
        for hh in range(2):
            b0, b1_ = a_blk[2 * zp, hh].astype(F32), a_blk[2 * zp + 1, hh].astype(F32)
            for ah in range(2):
                both = jnp.concatenate([b0[ah * 24 : ah * 24 + 24], b1_[ah * 24 : ah * 24 + 24]], axis=0)
                both = both.astype(BF16)
                cols = slice(ah * 512, (ah + 1) * 512)
                r = zp * 48
                split = min(max(128 - r, 0), 48)
                if split > 0:
                    a_all[hh * 128 + r : hh * 128 + r + split, cols] = both[:split]
                if split < 48:
                    start = 256 + hh * 64 + r + split - 128
                    a_all[start : start + 48 - split, cols] = both[split:]

    wait_recv(b_all.at[h, col_id(l, 1 - k)], fw_ss.at[7], fw_rs.at[7])
    for n, (dh, dl) in enumerate(y_offsets):
        hs, ls = (h + dh) % NH, (l - dl + NL) % NL
        wait_recv(b_all.at[hs, col_id(ls, 1 - k)], fw_ss.at[n], fw_rs.at[n])
    for n in range(8):
        bt_all[n, :, 0:128] = b_all[0, n, 0:256]
        bt_all[n, :, 128:256] = b_all[1, n, 0:256]
        f0, f1 = b_all[0, n, 256:384].astype(F32), b_all[1, n, 256:384].astype(F32)
        bt_all[n, 0:128, 256:384] = jnp.where(low, f0, pltpu.roll(f1, 64, 1)).astype(BF16)
        bt_all[n, 128:256, 256:384] = jnp.where(low, pltpu.roll(f0, 64, 1), f1).astype(BF16)

    @pl.loop(0, 8)
    def _(i):
        lhs = bt_all[:, pl.ds(pl.multiple_of(i * 32, 32), 32), :].reshape(256, 384)
        prod = jnp.dot(lhs, a_all[...], preferred_element_type=F32)
        prod = prod.reshape(8, 4, 8, 1024)
        for pair in range(2):
            p0 = prod[:, 2 * pair].reshape(64, 1024)
            p1 = prod[:, 2 * pair + 1].reshape(64, 1024)
            lanes = pl.ds(pl.multiple_of(i * 256 + pair * 128, 128), 128)
            for j in range(8):
                q0, q1 = p0[:, j * 128 : (j + 1) * 128], p1[:, j * 128 : (j + 1) * 128]
                e = jnp.where(low, q0, pltpu.roll(q1, 64, 1)).astype(BF16)
                o = jnp.where(low, pltpu.roll(q0, 64, 1), q1).astype(BF16)
                row = ((j % 2) * 8 + (j // 2) * 2) * 64
                integral[row : row + 64, lanes] = e
                integral[row + 64 : row + 128, lanes] = o

    for s in range(1, NX):
        wait_recv(t_all.at[(x - s + NX) % NX], t_ss.at[s], t_rs.at[s])

    def contract(which):
        rows = pl.ds(pl.multiple_of(which * 512, 512), 512)
        total = jnp.zeros((512, 256), F32)
        for n in range(NX):
            total += jnp.dot(
                integral[rows, n * 512 : (n + 1) * 512], t_all[n], preferred_element_type=F32
            )
        return total

    put(acc_p, contract(1 - k))
    cs = []
    for n in range(NX):
        c_send[n] = strided(acc_p, n, 128, 4).astype(BF16)
        cs.append(remote(c_send.at[n], c_recv.at[n], c_ss.at[n], c_rs.at[n], sibling))
        cs[-1].start()
    put(acc_o, contract(k))
    for n in range(NX):
        wait_recv(c_recv.at[n], c_ss.at[n], c_rs.at[n])
    xs = []
    for s in range(1, NX):
        xt = (x + s) % NX
        value = strided(acc_o, xt, 128, 4) + c_recv[xt].astype(F32)
        x_send[s] = value.astype(BF16)
        xs.append(remote(x_send.at[s], x_recv.at[s], x_ss.at[s], x_rs.at[s], at(x_=xt)))
        xs[-1].start()
    own = strided(acc_o, x, 128, 4) + c_recv[x].astype(F32)
    for s in range(1, NX):
        wait_recv(x_recv.at[s], x_ss.at[s], x_rs.at[s])
        own += x_recv[s].astype(F32)
    put(s_v, own)
    zs_ = []
    for s in range(1, NZ):
        zt = (z + s) % NZ
        z_send[s] = strided(s_v, zt, 16, 8).astype(BF16)
        zs_.append(remote(z_send.at[s], z_recv.at[s], z_ss.at[s], z_rs.at[s], at(z_=zt)))
        zs_[-1].start()
    own = strided(s_v, z, 16, 8)
    for s in range(1, NZ):
        wait_recv(z_recv.at[s], z_ss.at[s], z_rs.at[s])
        own += z_recv[s].astype(F32)
    put(s2_v, own)
    ys_ = []
    for n, (dh, dl) in enumerate(y_offsets):
        hd, ld = (h + dh) % NH, (l + dl) % NL
        y_send[n] = strided(s2_v, ld * 4 + hd, 2, 2)
        ys_.append(remote(y_send.at[n], y_recv.at[n], y_ss.at[n], y_rs.at[n], at(h_=hd, l_=ld)))
        ys_[-1].start()
    pair = lanes_of((1, 256))
    energy = jnp.zeros((1, 256), F32)
    for n in range(16):
        energy += jnp.where(pair // 16 == n, oo[n], 0.0) + jnp.where(pair % 16 == n, oo[n], 0.0)
    own = strided(s2_v, l * 4 + h, 2, 2)
    for n in range(len(y_offsets)):
        wait_recv(y_recv.at[n], y_ss.at[n], y_rs.at[n])
        own += y_recv[n]
    for j in range(2):
        out[j] = own[j : j + 1] / (oa[j] + ob[0] - energy)

    for copy in b1 + [am] + a_sent + ts + b2 + fw + cs + xs + zs_ + ys_:
        copy.wait_send()


def body(fa, fb, fo, sa, sb, tau, oa, ob, oo):
    vmem = pl.BlockSpec(memory_space=pltpu.VMEM)
    smem = pl.BlockSpec(memory_space=pltpu.SMEM)
    hbm = pl.BlockSpec(memory_space=pl.ANY)
    dma = pltpu.SemaphoreType.DMA
    scratch = [
        pltpu.VMEM((384, 512), F32),
        pltpu.VMEM((4, 192, 128), F32),
        pltpu.VMEM((2, 384, 128), F32),
        pltpu.VMEM((512, 256), BF16),
        pltpu.VMEM((2, 512, 128), F32),
        pltpu.VMEM((8, 48, 256), BF16),
        pltpu.VMEM((8, 48, 256), BF16),
        pltpu.VMEM((2, 384, 128), BF16),
        pltpu.VMEM((2, 8, 384, 128), BF16),
        pltpu.VMEM((8, 256, 384), BF16),
        pltpu.VMEM((8, 2, 48, 512), BF16),
        pltpu.VMEM((48, 512), BF16),
        pltpu.VMEM((384, 1024), BF16),
        pltpu.VMEM((4, 512, 256), BF16),
        pltpu.VMEM((1024, 2048), BF16),
        pltpu.VMEM((2, 512, 128), F32),
        pltpu.VMEM((2, 512, 128), F32),
        pltpu.VMEM((4, 128, 256), BF16),
        pltpu.VMEM((4, 128, 256), BF16),
        pltpu.VMEM((4, 128, 256), BF16),
        pltpu.VMEM((4, 128, 256), BF16),
        pltpu.VMEM((2, 128, 128), F32),
        pltpu.VMEM((8, 16, 256), BF16),
        pltpu.VMEM((8, 16, 256), BF16),
        pltpu.VMEM((2, 16, 128), F32),
        pltpu.VMEM((8, 2, 256), F32),
        pltpu.VMEM((8, 2, 256), F32),
        dma((8,)),
        dma((8,)), dma((8,)),
        dma((8,)), dma((8,)),
        dma((8,)), dma((8,)),
        dma((1,)), dma((1,)),
        dma((2, 8)), dma((2, 8)),
        dma((4,)), dma((4,)),
        dma((4,)), dma((4,)),
        dma((4,)), dma((4,)),
        dma((8,)), dma((8,)),
        dma((8,)), dma((8,)),
    ]
    return pl.pallas_call(
        kernel,
        out_shape=jax.ShapeDtypeStruct((2, 1, 256), F32),
        in_specs=[hbm, hbm, hbm, vmem, vmem, hbm, smem, smem, smem],
        out_specs=vmem,
        scratch_shapes=scratch,
        compiler_params=pltpu.CompilerParams(
            collective_id=0, has_side_effects=True, vmem_limit_bytes=60 * 1024 * 1024
        ),
        name="ladder",
    )(
        fa.reshape(384, 512),
        fb.reshape(192, 512),
        fo.reshape(384, 512),
        sa,
        sb,
        tau.reshape(512, 256),
        oa,
        ob,
        oo,
    )


def solution(mesh):
    return jax.shard_map(
        body,
        mesh=mesh,
        in_specs=(
            P("dev", None, None),
            P("dev", "col", None),
            P("dev", None, None),
            P(),
            P(None, "col"),
            P("col", "dev", None),
            P("col"),
            P("dev"),
            P(),
        ),
        out_specs=P("col", "dev", None),
        check_vma=False,
    )
```

time: 715 us -> 70.1 us (0.10)
  waiting for transfers between devices: 528 us -> 0 us
  blocking collectives: 128 us -> 0 us
  Pallas kernels: 0 us -> 66.6 us
  local copies, waits for them, and re-layouts: 28.2 us -> 2.57 us
  matrix products: 14.5 us -> 0 us
  between operations: 14.5 us -> 0.67 us
    reduce_scatter x1 -> x0, waiting for transfers between devices: 390 us -> none  [body(): lax.psum_scatter(partial_value, 'dev', scatter_dimension=1, tiled=True)]
    all_gather x2 -> x0, waiting for transfers between devices: 138 us -> none  [the longest x1 96.4 us: body(): whole_a = lax.all_gather(dressed_a, 'dev', axis=0, tiled=True)]
    unnamed x1 -> x0, blocking collectives: 74.7 us -> none
    pallas_call x0 -> x1, Pallas kernels: none -> 66.6 us  [body(): pl.pallas_call(kernel, out_shape=jax.ShapeDtypeStruct((2, 1, 256), F32),...]
    all_to_all x1 -> x0, blocking collectives: 53.7 us -> none  [body(): lax.all_to_all(grouped, 'dev', split_axis=1, concat_axis=0, tiled=True)]
    dot_general x4 -> x0, matrix products: 14.5 us -> none  [the longest x1 6.81 us: body(): jnp.dot(integral, doubles.reshape(c_tile * d_tile, pair_count), preferred...]
    transpose x2 -> x0, local copies, waits for them, and re-layouts: 12 us -> none  [the longest x1 6.56 us: body(): jnp.transpose(integral, (0, 2, 1, 3))]
    reshape x3 -> x0, local copies, waits for them, and re-layouts: 7.56 us -> none  [the longest x1 3.87 us: body(): jnp.transpose(grouped, (0, 2, 1, 3))]
  transfers between devices with their start and end apart: 3 -> 0, of which waited for: 3 -> 0; matrix products, arithmetic and copies ran while one was open for 2% -> 0% of each run, Pallas kernels for 0% -> 0%
where the time goes in v1:
time: 70.1 us; the launch traced here: 69.8 us
  Pallas kernels  66.6 us (95%)
  local copies, waits for them, and re-layouts  2.57 us (4%)
    pallas_call x1, Pallas kernels, body(): pl.pallas_call(kernel, out_shape=jax.ShapeDtypeStruct((2, 1, 256), F32),...  66.6 us
    unnamed x4, local copies, waits for them, and re-layouts  2.57 us

profile of v1, /device:TPU:1, one launch (start us, length us, event | category | flops | bytes accessed | tf_op | source)
XLA Modules:
  0.0 69.8 jit_solution(11560718474669782131)
XLA Ops:
  0.7 0.0 copy-start
  0.7 0.7 copy-done
  1.3 0.7 copy.10.sb
  2.0 66.6 %ladder.1 = f32[2,1,256]{2,1,0:T(1,128)} custom-call(f32[384,512]{1,0:T(8,128)} %bitcast.4, f32[192,512]{1,0:T(8,128)} %bitcast.6, f32[384,512]{1,0:T(8,128)} %bitcast.5, f32[16,16]{1,0:T(8,128)} %sa.1, f32[16,8]{1,0:T(8,128)} %copy.10.sb, bf16[512,256]{1,0:T(8,128)(2,1)} %bitcast.7, f32[2]{0:T(128)} %oa.1, f32[1]{0:T(128)S(6)} %copy.12.ob, f32[16]{0:T(128)} %oo.1), custom_call_target="tpu_custom_call" | custom-call | tf_op jit(solution)/shard_map/ladder/pallas_call | solution.py:404
  68.6 1.2 %copy.13 = f32[2,1,256]{2,1,0:T(1,128)} copy(f32[2,1,256]{2,1,0:T(1,128)} %ladder.1) | data formatting | bytes 4096
Async XLA Ops:
  0.7 0.7 copy-start

commit v2 on v1

v2 whole, which is shorter than its diff:
```python
import jax
import jax.numpy as jnp
from jax import lax
from jax.experimental import pallas as pl
from jax.experimental.pallas import tpu as pltpu
from jax.sharding import PartitionSpec as P

MESH = pl.DeviceIdType.MESH
F32 = jnp.float32
BF16 = jnp.bfloat16
HIGHEST = lax.Precision.HIGHEST
NH, NZ, NX, NL, NK = 2, 8, 4, 4, 2


def lanes_of(shape):
    return lax.broadcasted_iota(jnp.int32, shape, len(shape) - 1)


def rows_of(shape):
    return lax.broadcasted_iota(jnp.int32, shape, 0)


def spread(singles, rows):
    pick = (rows_of((rows * 8, rows)) // 8 == lanes_of((rows * 8, rows))).astype(F32)
    across = (rows_of((16, 128)) == lanes_of((16, 128)) % 16).astype(F32)
    first = lax.dot_general(pick, singles, (((1,), (0,)), ((), ())), precision=HIGHEST)
    full = jnp.dot(first, across, precision=HIGHEST)
    same = rows_of((rows * 8, 128)) % 8 == lanes_of((rows * 8, 128)) // 16
    return jnp.where(same, full, 0.0)


def strided(ref, start, size, stride):
    tiles = [ref[t, pl.ds(start, size, stride=stride), :] for t in range(ref.shape[0])]
    return jnp.concatenate(tiles, axis=1)


def put(ref, value):
    for t in range(ref.shape[0]):
        ref[t] = value[:, t * 128 : (t + 1) * 128]


def kernel(
    fa, fb, fo, sa, sb, tau, oa, ob, oo, out,
    fo_v, fb_v, fa_v, tau_v, tf_v,
    b1_send, b1_recv, b2_send, b_all,
    a_blk, a_mir, a_all, t_all, integral, acc,
    c_send, c_recv, x_send, x_recv, s_v, z_send, z_recv, s2_v, y_recv,
    load_sem, b1_ss, b1_rs, b2_ss, b2_rs, rl_ss, rl_rs, fw_ss, fw_rs, am_ss, am_rs, a_ss, a_rs,
    t_ss, t_rs, c_ss, c_rs, x_ss, x_rs, z_ss, z_rs, y_ss, y_rs,
):
    col = lax.axis_index("col")
    dev = lax.axis_index("dev")
    l, k = col // NK, col % NK
    h, z, x = dev // (NZ * NX), (dev // NX) % NZ, dev % NX
    sent = []

    def col_id(l_, k_):
        return l_ * NK + k_

    def at(h_=h, z_=z, x_=x, l_=l, k_=k):
        return (col_id(l_, k_), (h_ * NZ + z_) * NX + x_)

    def remote(src, dst, ss, rs, target):
        return pltpu.make_async_remote_copy(
            src_ref=src, dst_ref=dst, send_sem=ss, recv_sem=rs, device_id=target, device_id_type=MESH
        )

    def send(src, dst, ss, rs, target):
        copy = remote(src, dst, ss, rs, target)
        copy.start()
        sent.append(copy)

    def flush():
        while sent:
            sent.pop().wait_send()

    sibling = at(k_=1 - k)

    def wait_recv(dst, ss, rs):
        remote(dst, dst, ss, rs, sibling).wait_recv()

    ml = NL - 1 - l
    own_lanes = pl.ds(pl.multiple_of(l * 128, 128), 128)
    mir_lanes = pl.ds(pl.multiple_of(ml * 128, 128), 128)
    loads = [
        pltpu.make_async_copy(fo, fo_v, load_sem.at[0]),
        pltpu.make_async_copy(fa.at[:, mir_lanes], fa_v.at[0], load_sem.at[5]),
        pltpu.make_async_copy(fa.at[:, own_lanes], fa_v.at[1], load_sem.at[6]),
        pltpu.make_async_copy(tau, tau_v, load_sem.at[7]),
    ]
    loads[1:1] = [
        pltpu.make_async_copy(fb.at[:, t * 128 : (t + 1) * 128], fb_v.at[t], load_sem.at[1 + t])
        for t in range(4)
    ]
    for load in loads:
        load.start()

    y_offsets = [(e, f) for e in range(NH) for f in range(NL) if (e, f) != (0, 0)]
    everyone = [at(z_=(z + s) % NZ) for s in range(1, NZ)]
    everyone += [at(x_=(x + s) % NX) for s in range(1, NX)]
    everyone += [at(h_=(h + e) % NH, l_=(l + f) % NL) for e, f in y_offsets]
    everyone += [sibling]
    barrier = pltpu.get_barrier_semaphore()
    for peer in everyone:
        pl.semaphore_signal(barrier, inc=1, device_id=peer, device_id_type=MESH)

    lane128 = lanes_of((1, 128))
    low = lane128 < 64
    low16 = lanes_of((16, 128)) < 64

    pb = spread(sb[...], 8)
    for load in loads[:5]:
        load.wait()
    parts = [[] for _ in range(8)]
    for g in range(3):
        prod = jnp.dot(pb, fo_v[g * 128 : (g + 1) * 128, :], precision=HIGHEST)
        for b in range(8):
            parts[b].append(strided(fb_v, g * 64 + b, 8, 8) - prod[b * 8 : (b + 1) * 8])
    stacked = []
    for b in range(8):
        whole = jnp.concatenate(parts[b], axis=0)
        stacked.append(jnp.concatenate([whole[:, t * 128 : (t + 1) * 128] for t in range(4)], axis=0))
    quarter = lane128 % 64 < 32
    eighth = lane128 % 32 < 16
    ys = []
    for bq in range(2):
        x0, x1, x2, x3 = stacked[bq * 4 : bq * 4 + 4]
        u0 = jnp.where(low, x0, pltpu.roll(x2, 64, 1))
        u2 = jnp.where(low, pltpu.roll(x0, 64, 1), x2)
        u1 = jnp.where(low, x1, pltpu.roll(x3, 64, 1))
        u3 = jnp.where(low, pltpu.roll(x1, 64, 1), x3)
        ys.append([
            jnp.where(quarter, u0, pltpu.roll(u1, 32, 1)),
            jnp.where(quarter, pltpu.roll(u0, 96, 1), u1),
            jnp.where(quarter, u2, pltpu.roll(u3, 32, 1)),
            jnp.where(quarter, pltpu.roll(u2, 96, 1), u3),
        ])
    for j in range(4):
        y0, y1 = ys[0][j], ys[1][j]
        halves = (
            jnp.where(eighth, y0, pltpu.roll(y1, 16, 1)),
            jnp.where(eighth, pltpu.roll(y0, 112, 1), y1),
        )
        for c in range(2):
            for tt in range(2):
                y = halves[c]
                piece = jnp.concatenate(
                    [y[tt * 24 : tt * 24 + 24], y[(2 + tt) * 24 : (2 + tt) * 24 + 24]], axis=0
                )
                b1_send[c, tt * 4 + j] = piece.astype(BF16)

    pl.semaphore_wait(barrier, len(everyone))

    for c in range(2):
        for s in range(1, NZ):
            zt = (z + s) % NZ
            send(b1_send.at[c, zt], b1_recv.at[c, z], b1_ss.at[c, s], b1_rs.at[c, s], at(z_=zt))
        b1_recv[c, z] = b1_send[c, z]

    pa = spread(sa[...].T, 16)

    def dress_a(which):
        half = [[], []]
        for g in range(3):
            lanes = mir_lanes if which == 0 else own_lanes
            prod = jnp.dot(pa, fo_v[g * 128 : (g + 1) * 128, lanes], precision=HIGHEST)
            rows = []
            for a in range(16):
                d = fa_v[which, pl.ds(g * 128 + a, 8, stride=16), :] - prod[a * 8 : (a + 1) * 8]
                rows.append(d)
            for ah in range(2):
                lane_tiles = []
                for pair in range(4):
                    d0, d1 = rows[ah * 8 + pair * 2], rows[ah * 8 + pair * 2 + 1]
                    r0, r1 = pltpu.roll(d0, 64, 1), pltpu.roll(d1, 64, 1)
                    e0 = jnp.where(k == 0, d0, r0)
                    e1 = jnp.where(k == 0, r1, d1)
                    lane_tiles.append(jnp.where(low, e0, e1))
                half[ah].append(jnp.concatenate(lane_tiles, axis=1))
        return jnp.concatenate(half[0] + half[1], axis=0).astype(BF16)

    kinds = [1, -1, 2, -2, 3, -3, 4]

    def a_send(source, part, kind, by):
        ref = a_blk.at[source % NZ, h if part == 0 else 1 - h]
        n = kinds.index(kind)
        send(ref, ref, a_ss.at[part, n], a_rs.at[part, n], at(z_=(z + by + NZ) % NZ))

    def a_wait(part, kind):
        ref = a_blk.at[(z - kind + NZ) % NZ, h if part == 0 else 1 - h]
        n = kinds.index(kind)
        wait_recv(ref, a_ss.at[part, n], a_rs.at[part, n])

    def a_first(part):
        for kind in (2, -2, 1, -1):
            a_send(z, part, kind, kind)

    def a_second(part):
        a_wait(part, 2)
        a_send(z - 2 + NZ, part, 3, 1)
        if part == 0:
            a_send(z - 2 + NZ, part, 4, 2)
        a_wait(part, -2)
        a_send(z + 2, part, -3, -1)
        if part == 1:
            a_send(z + 2, part, 4, -2)

    loads[5].wait()
    a_mir[...] = dress_a(0)
    send(a_mir, a_blk.at[z, h], am_ss.at[0], am_rs.at[0], at(h_=1 - h, l_=ml))
    loads[6].wait()
    a_blk[z, h] = dress_a(1)
    a_first(0)

    loads[7].wait()
    put(tf_v, tau_v[...].astype(F32))
    for d in range(8):
        for e in range(2):
            t_all[x, d * 64 + e * 32 : d * 64 + e * 32 + 32, :] = strided(
                tf_v, e * 256 + d, 32, 8
            ).astype(BF16)
    for s in range(1, NX):
        ref = t_all.at[x]
        send(ref, ref, t_ss.at[s], t_rs.at[s], at(x_=(x + s) % NX))

    ri, ci = rows_of((128, 128)), lanes_of((128, 128))
    perm = ((ri // 8 == ci % 16) & (ri % 8 == (ci % 32) // 16 * 4 + ci // 32)).astype(BF16)

    def b_second(c):
        for s in range(1, NZ):
            wait_recv(b1_recv.at[c, (z - s + NZ) % NZ], b1_ss.at[c, s], b1_rs.at[c, s])
        blocks = [b1_recv[c, zz].astype(F32) for zz in range(NZ)]
        for hd in range(NH):
            rows = [blk[hd * 24 : hd * 24 + 24] for blk in blocks] + [jnp.zeros((64, 128), F32)]
            stack = jnp.concatenate(rows, axis=0).astype(BF16)
            bt = lax.dot_general(perm, stack, (((1,), (1,)), ((), ())), preferred_element_type=F32)
            rest = bt[:, 128:]
            fold = jnp.where(low, rest[:64], pltpu.roll(rest[64:], 64, 1))
            b2_send[c, hd, 0:128] = bt[:, :128].astype(BF16)
            b2_send[c, hd, 128:192] = fold.astype(BF16)
        for n, (hd, ld) in enumerate([(h, 2 - p), (h, partner), (1 - h, i0), (1 - h, 3 - i3)]):
            slot = (n // 2) * NL + l
            target = at(h_=hd, l_=ld)
            send(b2_send.at[c, hd], b_all.at[c, h, col], b2_ss.at[c, n], b2_rs.at[c, slot], target)
        send(b2_send.at[c, h], b_all.at[c, h, col], fw_ss.at[c, 0], fw_rs.at[c, l], sibling)
        b_all[c, h, col] = b2_send[c, h]

    p = l // 2
    partner = l + 1 - 2 * (l % 2)
    i0, i3 = (NL - 1 - l) // 3, l // 3

    def direct(l_):
        outer = ((l_ + 1) // 2 + 1) % 2
        right = l_ // 2
        named = []
        for n in range(3):
            left = outer * (3 - n) + (1 - outer) * (2, 3, 0)[n]
            half = outer + (1 - outer) * (0, 0, 1)[n]
            named.append((half, left * (1 - right) + (3 - left) * right))
        return named

    def b_block(c, name, k_):
        return b_all.at[c, (h + name[0]) % NH, col_id(name[1], k_)]

    def b_forward(c, name, n):
        ref = b_block(c, name, k)
        send(ref, ref, fw_ss.at[c, n], fw_rs.at[c, name[0] * NL + name[1]], sibling)

    def b_direct(c):
        for n, name in enumerate([(0, partner)] + direct(l)):
            ref = b_block(c, name, k)
            slot = name[0] * NL + name[1]
            wait_recv(ref, b2_ss.at[c, 0], b2_rs.at[c, slot])
            if n > 0:
                send(ref, ref, rl_ss.at[c, n], rl_rs.at[c, slot], at(l_=partner))
            b_forward(c, name, 1 + n)

    def b_relayed(c):
        for n, name in enumerate(direct(partner)):
            slot = name[0] * NL + name[1]
            wait_recv(b_block(c, name, k), rl_ss.at[c, 0], rl_rs.at[c, slot])
            b_forward(c, name, 5 + n)

    def b_forwarded(c):
        for half in range(NH):
            for l_ in range(NL):
                wait_recv(b_block(c, (half, l_), 1 - k), fw_ss.at[c, 0], fw_rs.at[c, half * NL + l_])

    b_second(0)
    b_second(1)
    wait_recv(a_blk.at[z, 1 - h], am_ss.at[0], am_rs.at[0])
    a_first(1)
    b_direct(0)
    a_second(0)
    b_relayed(0)
    a_second(1)
    b_direct(1)
    for part in range(2):
        for kind in (1, -1, 3, -3, 4):
            a_wait(part, kind)
    for zp in range(4):
        for hh in range(2):
            b0, b1 = a_blk[2 * zp, hh].astype(F32), a_blk[2 * zp + 1, hh].astype(F32)
            for ah in range(2):
                both = jnp.concatenate([b0[ah * 24 : ah * 24 + 24], b1[ah * 24 : ah * 24 + 24]], axis=0)
                both = both.astype(BF16)
                cols = slice(ah * 512, (ah + 1) * 512)
                r = zp * 48
                split = min(max(128 - r, 0), 48)
                if split > 0:
                    a_all[hh * 128 + r : hh * 128 + r + split, cols] = both[:split]
                if split < 48:
                    start = 256 + hh * 64 + r + split - 128
                    a_all[start : start + 48 - split, cols] = both[split:]

    def unit(c, u):
        rows = []
        for g in range(2):
            lg = 2 * u + g
            for kk in range(NK):
                m = col_id(lg, kk)
                m0, m1 = b_all[c, 0, m, 0:128], b_all[c, 1, m, 0:128]
                f0, f1 = b_all[c, 0, m, 128:192].astype(F32), b_all[c, 1, m, 128:192].astype(F32)
                top = jnp.where(low, f0, pltpu.roll(f1, 64, 1))
                bottom = jnp.where(low, pltpu.roll(f0, 64, 1), f1)
                rest = jnp.concatenate([top, bottom], axis=0).astype(BF16)
                rows.append(jnp.concatenate([m0, m1, rest], axis=1))
        lhs = jnp.concatenate(rows, axis=0)
        for jj in range(4):
            whole = jnp.dot(lhs, a_all[:, jj * 256 : (jj + 1) * 256], preferred_element_type=F32)
            for j in (2 * jj, 2 * jj + 1):
                for g in range(2):
                    prod = whole[g * 256 : (g + 1) * 256, (j % 2) * 128 : (j % 2) * 128 + 128]
                    prod = prod.reshape(2, 16, 8, 128)
                    row = g * 256 + (j % 2) * 128 + (j // 2) * 32
                    for i in range(8):
                        q0 = prod[:, 2 * i].reshape(16, 128).astype(BF16)
                        q1 = prod[:, 2 * i + 1].reshape(16, 128).astype(BF16)
                        e = jnp.where(low16, q0, pltpu.roll(q1, 64, 1))
                        o = jnp.where(low16, pltpu.roll(q0, 64, 1), q1)
                        integral[row : row + 16, i * 128 : (i + 1) * 128] = e
                        integral[row + 16 : row + 32, i * 128 : (i + 1) * 128] = o
        total = jnp.dot(integral[:, 0:512], t_all[2 * c], preferred_element_type=F32)
        total += jnp.dot(integral[:, 512:1024], t_all[2 * c + 1], preferred_element_type=F32)
        for g in range(2):
            for t in range(2):
                part = total[g * 256 : (g + 1) * 256, t * 128 : (t + 1) * 128]
                acc[2 * u + g, t] = part if c == 0 else acc[2 * u + g, t] + part

    for s in range(1, NX):
        wait_recv(t_all.at[(x - s + NX) % NX], t_ss.at[s], t_rs.at[s])
    b_forwarded(0)
    unit(0, 0)
    b_relayed(1)
    unit(0, 1)
    b_forwarded(1)

    def mine(u, half, x_):
        return jnp.concatenate([strided(acc.at[2 * u + g], half * 128 + x_, 32, 4) for g in range(2)], axis=0)

    def core_send(u):
        for x_ in range(NX):
            c_send[u, x_] = mine(u, 1 - k, x_).astype(BF16)
        send(c_send.at[u], c_recv.at[u], c_ss.at[u], c_rs.at[u], sibling)

    def x_exchange(u):
        wait_recv(c_recv.at[u], c_ss.at[u], c_rs.at[u])
        for n in range(1, NX):
            x_ = (x + n) % NX
            x_send[u, n] = (mine(u, k, x_) + c_recv[u, x_].astype(F32)).astype(BF16)
            send(x_send.at[u, n], x_recv.at[u, n], x_ss.at[u, n], x_rs.at[u, n], at(x_=x_))

    def x_sum(u):
        own = mine(u, k, x) + c_recv[u, x].astype(F32)
        for n in range(1, NX):
            wait_recv(x_recv.at[u, n], x_ss.at[u, n], x_rs.at[u, n])
            own += x_recv[u, n].astype(F32)
        for g in range(2):
            put(s_v.at[2 * u + g], own[g * 32 : g * 32 + 32])

    unit(1, 0)
    core_send(0)
    unit(1, 1)
    core_send(1)
    flush()
    x_exchange(0)
    x_exchange(1)
    x_sum(0)
    x_sum(1)

    def rows_for(z_):
        both = [strided(s_v.at[2 * half + z_ // 4], z_ % 4, 8, 4) for half in range(NH)]
        return jnp.concatenate(both, axis=0)

    for n in range(1, NZ):
        z_ = (z + n) % NZ
        z_send[n] = rows_for(z_).astype(BF16)
        send(z_send.at[n], z_recv.at[n], z_ss.at[n], z_rs.at[n], at(z_=z_))
    own = rows_for(z)
    flush()
    for n in range(1, NZ):
        wait_recv(z_recv.at[n], z_ss.at[n], z_rs.at[n])
        own += z_recv[n].astype(F32)
    for n in range(8):
        s2_v[n] = own[2 * n : 2 * n + 2]
    for n, (e, f) in enumerate(y_offsets):
        h_, l_ = (h + e) % NH, (l + f) % NL
        send(s2_v.at[h_ * NL + l_], y_recv.at[n], y_ss.at[n], y_rs.at[n], at(h_=h_, l_=l_))
    lane256 = lanes_of((1, 256))
    energy = jnp.zeros((1, 256), F32)
    for n in range(16):
        energy += jnp.where(lane256 // 16 == n, oo[n], 0.0) + jnp.where(lane256 % 16 == n, oo[n], 0.0)
    own = s2_v[h * NL + l]
    for n in range(len(y_offsets)):
        wait_recv(y_recv.at[n], y_ss.at[n], y_rs.at[n])
        own += y_recv[n]
    for j in range(2):
        out[j] = own[j : j + 1] / (oa[j] + ob[0] - energy)

    flush()


def body(fa, fb, fo, sa, sb, tau, oa, ob, oo):
    vmem = pl.BlockSpec(memory_space=pltpu.VMEM)
    smem = pl.BlockSpec(memory_space=pltpu.SMEM)
    hbm = pl.BlockSpec(memory_space=pl.ANY)
    dma = pltpu.SemaphoreType.DMA
    scratch = [
        pltpu.VMEM((384, 512), F32),
        pltpu.VMEM((4, 192, 128), F32),
        pltpu.VMEM((2, 384, 128), F32),
        pltpu.VMEM((512, 256), BF16),
        pltpu.VMEM((2, 512, 128), F32),
        pltpu.VMEM((2, 8, 48, 128), BF16),
        pltpu.VMEM((2, 8, 48, 128), BF16),
        pltpu.VMEM((2, 2, 192, 128), BF16),
        pltpu.VMEM((2, 2, 8, 192, 128), BF16),
        pltpu.VMEM((8, 2, 48, 512), BF16),
        pltpu.VMEM((48, 512), BF16),
        pltpu.VMEM((384, 1024), BF16),
        pltpu.VMEM((4, 512, 256), BF16),
        pltpu.VMEM((512, 1024), BF16),
        pltpu.VMEM((4, 2, 256, 128), F32),
        pltpu.VMEM((2, 4, 64, 256), BF16),
        pltpu.VMEM((2, 4, 64, 256), BF16),
        pltpu.VMEM((2, 4, 64, 256), BF16),
        pltpu.VMEM((2, 4, 64, 256), BF16),
        pltpu.VMEM((4, 2, 32, 128), F32),
        pltpu.VMEM((8, 16, 256), BF16),
        pltpu.VMEM((8, 16, 256), BF16),
        pltpu.VMEM((8, 2, 256), F32),
        pltpu.VMEM((8, 2, 256), F32),
        dma((8,)),
        dma((2, 8)), dma((2, 8)),
        dma((2, 8)), dma((2, 8)),
        dma((2, 8)), dma((2, 8)),
        dma((2, 8)), dma((2, 8)),
        dma((1,)), dma((1,)),
        dma((2, 7)), dma((2, 7)),
        dma((4,)), dma((4,)),
        dma((2,)), dma((2,)),
        dma((2, 4)), dma((2, 4)),
        dma((8,)), dma((8,)),
        dma((8,)), dma((8,)),
    ]
    return pl.pallas_call(
        kernel,
        out_shape=jax.ShapeDtypeStruct((2, 1, 256), F32),
        in_specs=[hbm, hbm, hbm, vmem, vmem, hbm, smem, smem, smem],
        out_specs=vmem,
        scratch_shapes=scratch,
        compiler_params=pltpu.CompilerParams(
            collective_id=0, has_side_effects=True, vmem_limit_bytes=60 * 1024 * 1024
        ),
        name="ladder",
    )(
        fa.reshape(384, 512),
        fb.reshape(192, 512),
        fo.reshape(384, 512),
        sa,
        sb.T,
        tau.reshape(512, 256),
        oa,
        ob,
        oo,
    )


def solution(mesh):
    return jax.shard_map(
        body,
        mesh=mesh,
        in_specs=(
            P("dev", None, None),
            P("dev", "col", None),
            P("dev", None, None),
            P(),
            P(None, "col"),
            P("col", "dev", None),
            P("col"),
            P("dev"),
            P(),
        ),
        out_specs=P("col", "dev", None),
        check_vma=False,
    )
```

time: 70.1 us -> 63.7 us (0.909)
  the two profiles are of different devices: /device:TPU:1 before, /device:TPU:48 now
where the time goes in v2:
time: 63.7 us; the launch traced here: 63.5 us
  Pallas kernels  61.6 us (97%)
  local copies, waits for them, and re-layouts  1.26 us (2%)
  between operations  0.66 us (1%)
    pallas_call x1, Pallas kernels, body(): pl.pallas_call(kernel, out_shape=jax.ShapeDtypeStruct((2, 1, 256), F32),...  61.6 us

profile of v2, /device:TPU:48, one launch (start us, length us, event | category | flops | bytes accessed | tf_op | source)
XLA Modules:
  0.0 63.5 jit_solution(15827205275486854169)
XLA Ops:
  0.7 61.6 %ladder.1 = f32[2,1,256]{2,1,0:T(1,128)} custom-call(f32[384,512]{1,0:T(8,128)} %bitcast.5, f32[192,512]{1,0:T(8,128)} %bitcast.7, f32[384,512]{1,0:T(8,128)} %bitcast.6, f32[16,16]{1,0:T(8,128)} %sa.1, f32[8,16]{1,0:T(8,128)} %bitcast.9, bf16[512,256]{1,0:T(8,128)(2,1)} %bitcast.8, f32[2]{0:T(128)} %oa.1, f32[1]{0:T(128)S(6)} %copy.11.ob, f32[16]{0:T(128)} %oo.1), custom_call_target="tpu_custom_call" | custom-call | tf_op jit(solution)/shard_map/ladder/pallas_call | solution.py:466
  62.3 1.3 %copy.12 = f32[2,1,256]{2,1,0:T(1,128)} copy(f32[2,1,256]{2,1,0:T(1,128)} %ladder.1) | data formatting | bytes 4096

commit v3 on v2

--- a/solution.py
+++ b/solution.py
@@ -45,7 +45,7 @@
     b1_send, b1_recv, b2_send, b_all,
     a_blk, a_mir, a_all, t_all, integral, acc,
     c_send, c_recv, x_send, x_recv, s_v, z_send, z_recv, s2_v, y_recv,
-    load_sem, b1_ss, b1_rs, b2_ss, b2_rs, rl_ss, rl_rs, fw_ss, fw_rs, am_ss, am_rs, a_ss, a_rs,
+    load_sem, b1_ss, b1_rs, b2_ss, b2_rs, fw_ss, fw_rs, am_ss, am_rs, a_ss, a_rs,
     t_ss, t_rs, c_ss, c_rs, x_ss, x_rs, z_ss, z_rs, y_ss, y_rs,
 ):
     col = lax.axis_index("col")
@@ -192,18 +192,15 @@
         wait_recv(ref, a_ss.at[part, n], a_rs.at[part, n])
 
     def a_first(part):
-        for kind in (2, -2, 1, -1):
+        for kind in (2, -2, 1, -1) if part == 0 else kinds:
             a_send(z, part, kind, kind)
 
-    def a_second(part):
-        a_wait(part, 2)
-        a_send(z - 2 + NZ, part, 3, 1)
-        if part == 0:
-            a_send(z - 2 + NZ, part, 4, 2)
-        a_wait(part, -2)
-        a_send(z + 2, part, -3, -1)
-        if part == 1:
-            a_send(z + 2, part, 4, -2)
+    def a_second():
+        a_wait(0, 2)
+        a_send(z - 2 + NZ, 0, 3, 1)
+        a_send(z - 2 + NZ, 0, 4, 2)
+        a_wait(0, -2)
+        a_send(z + 2, 0, -3, -1)
 
     loads[5].wait()
     a_mir[...] = dress_a(0)
@@ -238,65 +235,35 @@
             fold = jnp.where(low, rest[:64], pltpu.roll(rest[64:], 64, 1))
             b2_send[c, hd, 0:128] = bt[:, :128].astype(BF16)
             b2_send[c, hd, 128:192] = fold.astype(BF16)
-        for n, (hd, ld) in enumerate([(h, 2 - p), (h, partner), (1 - h, i0), (1 - h, 3 - i3)]):
-            slot = (n // 2) * NL + l
-            target = at(h_=hd, l_=ld)
-            send(b2_send.at[c, hd], b_all.at[c, h, col], b2_ss.at[c, n], b2_rs.at[c, slot], target)
-        send(b2_send.at[c, h], b_all.at[c, h, col], fw_ss.at[c, 0], fw_rs.at[c, l], sibling)
+        for n, (e, f) in enumerate(y_offsets):
+            hd = (h + e) % NH
+            target = at(h_=hd, l_=(l + f) % NL)
+            send(b2_send.at[c, hd], b_all.at[c, h, col], b2_ss.at[c, n], b2_rs.at[c, n], target)
+        send(b2_send.at[c, h], b_all.at[c, h, col], fw_ss.at[c, 7], fw_rs.at[c, 7], sibling)
         b_all[c, h, col] = b2_send[c, h]
 
-    p = l // 2
-    partner = l + 1 - 2 * (l % 2)
-    i0, i3 = (NL - 1 - l) // 3, l // 3
-
-    def direct(l_):
-        outer = ((l_ + 1) // 2 + 1) % 2
-        right = l_ // 2
-        named = []
-        for n in range(3):
-            left = outer * (3 - n) + (1 - outer) * (2, 3, 0)[n]
-            half = outer + (1 - outer) * (0, 0, 1)[n]
-            named.append((half, left * (1 - right) + (3 - left) * right))
-        return named
-
-    def b_block(c, name, k_):
-        return b_all.at[c, (h + name[0]) % NH, col_id(name[1], k_)]
-
-    def b_forward(c, name, n):
-        ref = b_block(c, name, k)
-        send(ref, ref, fw_ss.at[c, n], fw_rs.at[c, name[0] * NL + name[1]], sibling)
-
-    def b_direct(c):
-        for n, name in enumerate([(0, partner)] + direct(l)):
-            ref = b_block(c, name, k)
-            slot = name[0] * NL + name[1]
-            wait_recv(ref, b2_ss.at[c, 0], b2_rs.at[c, slot])
-            if n > 0:
-                send(ref, ref, rl_ss.at[c, n], rl_rs.at[c, slot], at(l_=partner))
-            b_forward(c, name, 1 + n)
-
-    def b_relayed(c):
-        for n, name in enumerate(direct(partner)):
-            slot = name[0] * NL + name[1]
-            wait_recv(b_block(c, name, k), rl_ss.at[c, 0], rl_rs.at[c, slot])
-            b_forward(c, name, 5 + n)
+    def b_block(c, n, k_):
+        e, f = y_offsets[n] if n < 7 else (0, 0)
+        return b_all.at[c, (h + e) % NH, col_id((l - f + NL) % NL, k_)]
+
+    def b_forward(c):
+        for n in range(7):
+            ref = b_block(c, n, k)
+            wait_recv(ref, b2_ss.at[c, n], b2_rs.at[c, n])
+            send(ref, ref, fw_ss.at[c, n], fw_rs.at[c, n], sibling)
 
     def b_forwarded(c):
-        for half in range(NH):
-            for l_ in range(NL):
-                wait_recv(b_block(c, (half, l_), 1 - k), fw_ss.at[c, 0], fw_rs.at[c, half * NL + l_])
+        for n in range(8):
+            wait_recv(b_block(c, n, 1 - k), fw_ss.at[c, n], fw_rs.at[c, n])
 
     b_second(0)
     b_second(1)
     wait_recv(a_blk.at[z, 1 - h], am_ss.at[0], am_rs.at[0])
     a_first(1)
-    b_direct(0)
-    a_second(0)
-    b_relayed(0)
-    a_second(1)
-    b_direct(1)
+    a_second()
+    b_forward(0)
     for part in range(2):
-        for kind in (1, -1, 3, -3, 4):
+        for kind in (1, -1, 3, -3, 4) if part == 0 else kinds:
             a_wait(part, kind)
     for zp in range(4):
         for hh in range(2):
@@ -351,7 +318,7 @@
         wait_recv(t_all.at[(x - s + NX) % NX], t_ss.at[s], t_rs.at[s])
     b_forwarded(0)
     unit(0, 0)
-    b_relayed(1)
+    b_forward(1)
     unit(0, 1)
     b_forwarded(1)
 
@@ -454,7 +421,6 @@
         dma((2, 8)), dma((2, 8)),
         dma((2, 8)), dma((2, 8)),
         dma((2, 8)), dma((2, 8)),
-        dma((2, 8)), dma((2, 8)),
         dma((1,)), dma((1,)),
         dma((2, 7)), dma((2, 7)),
         dma((4,)), dma((4,)),

time: 63.7 us -> 64.4 us (1.011)
  the two profiles are of different devices: /device:TPU:48 before, /device:TPU:1 now
where the time goes in v3:
time: 64.4 us; the launch traced here: 63.6 us
  Pallas kernels  61.7 us (96%)
  local copies, waits for them, and re-layouts  1.26 us (2%)
  between operations  0.66 us (1%)
    pallas_call x1, Pallas kernels, body(): pl.pallas_call(kernel, out_shape=jax.ShapeDtypeStruct((2, 1, 256), F32),...  61.7 us

profile of v3, /device:TPU:1, one launch (start us, length us, event | category | flops | bytes accessed | tf_op | source)
XLA Modules:
  0.0 63.6 jit_solution(780107485069052732)
XLA Ops:
  0.7 61.7 %ladder.1 = f32[2,1,256]{2,1,0:T(1,128)} custom-call(f32[384,512]{1,0:T(8,128)} %bitcast.5, f32[192,512]{1,0:T(8,128)} %bitcast.7, f32[384,512]{1,0:T(8,128)} %bitcast.6, f32[16,16]{1,0:T(8,128)} %sa.1, f32[8,16]{1,0:T(8,128)} %bitcast.9, bf16[512,256]{1,0:T(8,128)(2,1)} %bitcast.8, f32[2]{0:T(128)} %oa.1, f32[1]{0:T(128)S(6)} %copy.11.ob, f32[16]{0:T(128)} %oo.1), custom_call_target="tpu_custom_call" | custom-call | tf_op jit(solution)/shard_map/ladder/pallas_call | solution.py:432
  62.3 1.3 %copy.12 = f32[2,1,256]{2,1,0:T(1,128)} copy(f32[2,1,256]{2,1,0:T(1,128)} %ladder.1) | data formatting | bytes 4096

commit v4 on v2

--- a/solution.py
+++ b/solution.py
@@ -92,7 +92,7 @@
         pltpu.make_async_copy(fb.at[:, t * 128 : (t + 1) * 128], fb_v.at[t], load_sem.at[1 + t])
         for t in range(4)
     ]
-    for load in loads:
+    for load in loads[:5]:
         load.start()
 
     y_offsets = [(e, f) for e in range(NH) for f in range(NL) if (e, f) != (0, 0)]
@@ -103,6 +103,9 @@
     barrier = pltpu.get_barrier_semaphore()
     for peer in everyone:
         pl.semaphore_signal(barrier, inc=1, device_id=peer, device_id_type=MESH)
+
+    for load in loads[5:]:
+        load.start()
 
     lane128 = lanes_of((1, 128))
     low = lane128 < 64
@@ -281,9 +284,9 @@
             wait_recv(b_block(c, name, k), rl_ss.at[c, 0], rl_rs.at[c, slot])
             b_forward(c, name, 5 + n)
 
-    def b_forwarded(c):
+    def b_forwarded(c, u):
         for half in range(NH):
-            for l_ in range(NL):
+            for l_ in (2 * u, 2 * u + 1):
                 wait_recv(b_block(c, (half, l_), 1 - k), fw_ss.at[c, 0], fw_rs.at[c, half * NL + l_])
 
     b_second(0)
@@ -349,11 +352,12 @@
 
     for s in range(1, NX):
         wait_recv(t_all.at[(x - s + NX) % NX], t_ss.at[s], t_rs.at[s])
-    b_forwarded(0)
+    b_forwarded(0, 0)
     unit(0, 0)
+    b_forwarded(0, 1)
     b_relayed(1)
     unit(0, 1)
-    b_forwarded(1)
+    b_forwarded(1, 0)
 
     def mine(u, half, x_):
         return jnp.concatenate([strided(acc.at[2 * u + g], half * 128 + x_, 32, 4) for g in range(2)], axis=0)
@@ -380,11 +384,12 @@
 
     unit(1, 0)
     core_send(0)
+    b_forwarded(1, 1)
     unit(1, 1)
     core_send(1)
-    flush()
     x_exchange(0)
     x_exchange(1)
+    flush()
     x_sum(0)
     x_sum(1)
 

time: 63.7 us -> 63 us (0.989)
  the two profiles are of different devices: /device:TPU:48 before, /device:TPU:1 now
where the time goes in v4:
time: 63 us; the launch traced here: 62.7 us
  Pallas kernels  60.8 us (97%)
  local copies, waits for them, and re-layouts  1.26 us (2%)
  between operations  0.66 us (1%)
    pallas_call x1, Pallas kernels, body(): pl.pallas_call(kernel, out_shape=jax.ShapeDtypeStruct((2, 1, 256), F32),...  60.8 us
    unnamed x1, local copies, waits for them, and re-layouts  1.26 us

profile of v4, /device:TPU:1, one launch (start us, length us, event | category | flops | bytes accessed | tf_op | source)
XLA Modules:
  0.0 62.7 jit_solution(2868774347218299377)
XLA Ops:
  0.7 60.8 %ladder.1 = f32[2,1,256]{2,1,0:T(1,128)} custom-call(f32[384,512]{1,0:T(8,128)} %bitcast.5, f32[192,512]{1,0:T(8,128)} %bitcast.7, f32[384,512]{1,0:T(8,128)} %bitcast.6, f32[16,16]{1,0:T(8,128)} %sa.1, f32[8,16]{1,0:T(8,128)} %bitcast.9, bf16[512,256]{1,0:T(8,128)(2,1)} %bitcast.8, f32[2]{0:T(128)} %oa.1, f32[1]{0:T(128)S(6)} %copy.11.ob, f32[16]{0:T(128)} %oo.1), custom_call_target="tpu_custom_call" | custom-call | tf_op jit(solution)/shard_map/ladder/pallas_call | solution.py:471
  61.4 1.3 %copy.12 = f32[2,1,256]{2,1,0:T(1,128)} copy(f32[2,1,256]{2,1,0:T(1,128)} %ladder.1) | data formatting | bytes 4096

commit v5 on v4

--- a/solution.py
+++ b/solution.py
@@ -215,17 +215,6 @@
     a_blk[z, h] = dress_a(1)
     a_first(0)
 
-    loads[7].wait()
-    put(tf_v, tau_v[...].astype(F32))
-    for d in range(8):
-        for e in range(2):
-            t_all[x, d * 64 + e * 32 : d * 64 + e * 32 + 32, :] = strided(
-                tf_v, e * 256 + d, 32, 8
-            ).astype(BF16)
-    for s in range(1, NX):
-        ref = t_all.at[x]
-        send(ref, ref, t_ss.at[s], t_rs.at[s], at(x_=(x + s) % NX))
-
     ri, ci = rows_of((128, 128)), lanes_of((128, 128))
     perm = ((ri // 8 == ci % 16) & (ri % 8 == (ci % 32) // 16 * 4 + ci // 32)).astype(BF16)
 
@@ -291,6 +280,18 @@
 
     b_second(0)
     b_second(1)
+
+    loads[7].wait()
+    put(tf_v, tau_v[...].astype(F32))
+    for d in range(8):
+        for e in range(2):
+            t_all[x, d * 64 + e * 32 : d * 64 + e * 32 + 32, :] = strided(
+                tf_v, e * 256 + d, 32, 8
+            ).astype(BF16)
+    for s in range(1, NX):
+        ref = t_all.at[x]
+        send(ref, ref, t_ss.at[s], t_rs.at[s], at(x_=(x + s) % NX))
+
     wait_recv(a_blk.at[z, 1 - h], am_ss.at[0], am_rs.at[0])
     a_first(1)
     b_direct(0)

time: 63 us -> 63 us (level)
  no operation moved by 1% of the time
where the time goes in v5:
time: 63 us; the launch traced here: 62.7 us
  Pallas kernels  60.8 us (97%)
  local copies, waits for them, and re-layouts  1.26 us (2%)
  between operations  0.66 us (1%)
    pallas_call x1, Pallas kernels, body(): pl.pallas_call(kernel, out_shape=jax.ShapeDtypeStruct((2, 1, 256), F32),...  60.8 us
    unnamed x1, local copies, waits for them, and re-layouts  1.26 us

profile of v5, /device:TPU:1, one launch (start us, length us, event | category | flops | bytes accessed | tf_op | source)
XLA Modules:
  0.0 62.7 jit_solution(503897790144425277)
XLA Ops:
  0.7 60.8 %ladder.1 = f32[2,1,256]{2,1,0:T(1,128)} custom-call(f32[384,512]{1,0:T(8,128)} %bitcast.5, f32[192,512]{1,0:T(8,128)} %bitcast.7, f32[384,512]{1,0:T(8,128)} %bitcast.6, f32[16,16]{1,0:T(8,128)} %sa.1, f32[8,16]{1,0:T(8,128)} %bitcast.9, bf16[512,256]{1,0:T(8,128)(2,1)} %bitcast.8, f32[2]{0:T(128)} %oa.1, f32[1]{0:T(128)S(6)} %copy.11.ob, f32[16]{0:T(128)} %oo.1), custom_call_target="tpu_custom_call" | custom-call | tf_op jit(solution)/shard_map/ladder/pallas_call | solution.py:472
  61.4 1.3 %copy.12 = f32[2,1,256]{2,1,0:T(1,128)} copy(f32[2,1,256]{2,1,0:T(1,128)} %ladder.1) | data formatting | bytes 4096
